TPU v7x, 512 devices: a whole 4x8x8 slice. The times are simulated.
512 devices in a mesh: vol: 32 (over x, z), nar: 16 (over y, core).
Axes of the slice: x: 4, y: 8, z: 8, core: 2. Of those that a mesh axis runs over, the one named last changes fastest.
Arguments:
- series: bfloat16 [32768, 2048], P(('vol', 'nar')), may hold values from -6 to 6
- send_rows: int32 [32, 16, 64], P('vol', 'nar'), may hold values from -1 to 63, as said below
- bin_counts: int32 [16], replicated, may hold values from 1 to 32, 256 in all
- observer_cells: int32 [2, 512], replicated, may hold values from 0 to 127
Outputs:
- spectra_out: float32 [16, 32, 2, 512], P('nar', 'vol')
Inputs may be any that keep to these rules, and one draw needn't show every extreme that they name: `send_rows`: entry (u, n, k) names the row of device (u, n)'s 64 rows of series for slot k mod 2 bound for the patch owner at vol index k // 2 and nar index n, or is -1 for an empty slot; one device never names a row twice. Nar index m owns bin_counts[m] bins in order, from the sum of the counts before m on; some owner holds exactly 32 bins. `observer_cells`: row 0 holds polar indices, row 1 azimuthal indices.
All inputs are finite; a program needn't handle non-finite values.
Results may differ from a plain program's by a relative error of at most 0.0043.
Values may be sent and summed in bfloat16 or wider, within the bound.
A program may use at most 64 MiB of HBM per device.

v0:
```python
import math
import jax
import jax.numpy as jnp
from jax import lax
from jax.sharding import PartitionSpec as P

NF = 256
NQ = 4
WAVE_STEP = 0.05


def dft_table(bin_ids, keep_bin, time_len):
    time_steps = jnp.arange(time_len, dtype=jnp.int32)
    frequency = bin_ids + 1
    phase_turns = time_steps[:, None] * frequency[None, :] % time_len
    angle_grid = phase_turns.astype(jnp.float32) * (2.0 * math.pi / time_len)
    dft_grid = jnp.stack([jnp.cos(angle_grid), -jnp.sin(angle_grid)], axis=-1)
    dft_grid = jnp.where(keep_bin[None, :, None], dft_grid, jnp.float32(0.0))
    return dft_grid.reshape(time_len, 2 * bin_ids.shape[0]).astype(jnp.bfloat16)


def positions(point_list):
    beside_all = (point_list * 1597 % 8191).astype(jnp.float32) * (2.0 * math.pi / 8191.0)
    jitter = (point_list * 613 % 127).astype(jnp.float32) * (0.37 / 127.0)
    axial = (point_list // 128).astype(jnp.float32) * 0.5 + jitter
    return (20.0 * jnp.cos(beside_all), 20.0 * jnp.sin(beside_all), axial)


def directions(obs_cells):
    polar_angle = (obs_cells[0].astype(jnp.float32) + 0.5) * (math.pi / 128.0)
    azimuth = obs_cells[1].astype(jnp.float32) * (2.0 * math.pi / 128.0)
    return (
        jnp.sin(polar_angle) * jnp.cos(azimuth),
        jnp.sin(polar_angle) * jnp.sin(azimuth),
        jnp.cos(polar_angle),
    )


def project(facing, place_xyz):
    dotted = facing[0][:, None] * place_xyz[0][None, :] + facing[1][:, None] * place_xyz[1][None, :]
    return dotted + facing[2][:, None] * place_xyz[2][None, :]


def kernels(bin_ids, dotted):
    wavenumber = (bin_ids.astype(jnp.float32) + 1.0) * WAVE_STEP
    phase_grid = wavenumber[:, None, None] * dotted[None]
    return jnp.concatenate([jnp.cos(phase_grid), jnp.sin(phase_grid)], axis=1).astype(jnp.bfloat16)


def combine(products, bin_ids, facing, norm_scale):
    observers = facing[0].shape[0]
    bin_total = bin_ids.shape[0]
    cos_part = products[:, :observers].reshape(bin_total, observers, NQ, 2)
    sine_part = products[:, observers:].reshape(bin_total, observers, NQ, 2)
    real_part = cos_part[..., 0] + sine_part[..., 1]
    imag_part = cos_part[..., 1] - sine_part[..., 0]
    weights = jnp.stack([jnp.ones_like(facing[0]), facing[0], facing[1], facing[2]], axis=-1)
    real_sum = jnp.sum(real_part * weights[None], axis=-1)
    imag_sum = jnp.sum(imag_part * weights[None], axis=-1)
    amplitude = (bin_ids.astype(jnp.float32) + 1.0) * (norm_scale / NF)
    return jnp.stack([-amplitude[:, None] * imag_sum, amplitude[:, None] * real_sum], axis=1)


def apply_green(bin_ids, spec_block, dotted, facing, norm_scale):
    green_grid = kernels(bin_ids, dotted)
    products = jnp.einsum(
        "bxp,bcp->bxc", green_grid, spec_block, preferred_element_type=jnp.float32
    )
    return combine(products, bin_ids, facing, norm_scale)


def per_device(series, send_rows, bin_counts, observer_cells):
    vol_count = lax.axis_size("vol")
    nar_count = lax.axis_size("nar")
    vol_index = lax.axis_index("vol")
    nar_index = lax.axis_index("nar")
    bin_cap = vol_count * max(1, 2 * NF // (nar_count * vol_count))
    time_len = series.shape[1] // NQ
    slot_total = send_rows.shape[2]
    slot_width = slot_total // vol_count
    listing = send_rows.reshape(-1)
    picked = jnp.take(series, jnp.maximum(listing, 0), axis=0)
    packed = jnp.where((listing >= 0)[:, None], picked, jnp.zeros((), series.dtype))
    arrived = lax.all_to_all(packed, "vol", split_axis=0, concat_axis=0, tiled=True)
    owners = jnp.arange(bin_counts.shape[0], dtype=jnp.int32)
    starts = jnp.sum(jnp.where(owners[None, :] < owners[:, None], bin_counts[None, :], 0), axis=1)
    own_start = starts[nar_index]
    own_count = bin_counts[nar_index]
    dft_scale = 1.0 / math.sqrt(time_len)
    within = jnp.arange(bin_cap, dtype=jnp.int32)
    own_table = dft_table(own_start + within, within < own_count, time_len)
    row_piece = lax.all_gather(arrived, "nar", axis=0, tiled=True)
    rows_here = row_piece.shape[0]
    spectral = jnp.dot(
        row_piece.reshape(rows_here * NQ, time_len), own_table, preferred_element_type=jnp.float32
    )
    spectral = (spectral * dft_scale).astype(jnp.bfloat16).reshape(rows_here, NQ, bin_cap, 2)
    spectra = spectral.transpose(2, 1, 3, 0).reshape(bin_cap, 2 * NQ, rows_here)
    local_points = nar_count * slot_total
    norm_scale = 1.0 / math.sqrt(vol_count * nar_count * slot_total)
    facing = directions(observer_cells)
    share_rows = bin_cap // vol_count
    local_index = jnp.arange(local_points, dtype=jnp.int32)
    nar_source = local_index // slot_total
    remain = local_index % slot_total
    vol_source = remain // slot_width
    within_slot = remain % slot_width
    dotted = project(
        facing,
        positions(
            ((vol_source * nar_count + nar_source) * vol_count + vol_index) * slot_width
            + within_slot
        ),
    )
    row_count = lax.axis_size("vol") * share_rows
    bin_ids = own_start + jnp.arange(row_count, dtype=jnp.int32)
    group_size = 4

    def one_group(bundle):
        return apply_green(bundle[0], bundle[1], dotted, facing, norm_scale)

    grouped = lax.map(
        one_group,
        (
            bin_ids.reshape(row_count // group_size, group_size),
            spectra.reshape(row_count // group_size, group_size, 2 * NQ, local_points),
        ),
    )
    result = lax.psum_scatter(
        grouped.reshape(row_count, 2, grouped.shape[-1]), "vol", scatter_dimension=0, tiled=True
    )
    return result.reshape(1, share_rows, 2, result.shape[-1])


def solution(mesh):
    placed = (P(("vol", "nar"), None), P("vol", "nar", None), P(), P())
    return jax.shard_map(
        per_device,
        mesh=mesh,
        in_specs=placed,
        out_specs=P("nar", "vol", None, None),
        check_vma=False,
    )
```

profile of v0, /device:TPU:2, one launch (start us, length us, event | category | flops | bytes accessed | tf_op | source)
XLA Modules:
  0.0 570.2 jit_solution(7195838264246418794)
XLA Ops:
  6.5 0.7 compare_reduce_fusion
  7.3 0.7 maximum_bitcast_fusion.1
  7.9 0.1 ge.18
  8.0 0.1 le.17
  8.2 0.7 gather_fusion
  8.9 0.2 gather.7
  9.1 0.4 broadcast_select_fusion.1
  9.5 24.5 %all_to_all.9 = bf16[32,2,2048]{2,1,0:T(2,128)(2,1)S(1)} all-to-all(bf16[32,2,2048]{2,1,0:T(2,128)(2,1)S(1)} %broadcast_select_fusion.1), channel_id=1, replica_groups=mesh['vol'=32,'nar'=16] {'vol'}, dimensions={0} | all-to-all | bytes 524288 | tf_op jit(solution)/shard_map/all_to_all | solution.py:84
  34.1 0.8 all_to_all.7
  35.0 0.7 dynamic_slice.15
  35.6 0.1 select_reduce_fusion
  35.7 0.6 dynamic_slice.14
  36.4 0.6 add_add_fusion.1
  37.0 0.6 iota_compare_fusion.1
  37.6 0.3 fusion.27
  38.2 0.6 add_add_fusion
  39.0 0.1 fusion.58
  39.1 37.2 %all-gather.2.cloned.1.call-done = bf16[1024,2048]{1,0:T(8,128)(2,1)} async-done(((bf16[64,2048]{1,0:T(8,128)(2,1)}), bf16[1024,2048]{1,0:T(8,128)(2,1)}) %all-gather.2.cloned.1.call-update) | async-done | bytes 4194320 | tf_op jit(solution)/shard_map/all_gather | solution.py:92
  76.3 7.6 %reshape.422 = bf16[4096,512]{1,0:T(8,128)(2,1)} reshape(bf16[1024,2048]{1,0:T(8,128)(2,1)} %all-gather.2.cloned.1.call-done) | data formatting | bytes 8388608 | tf_op jit(solution)/shard_map/reshape | solution.py:95
  83.9 3.6 fusion.19
  87.5 37.2 %reshape.423 = bf16[1024,4,32,2]{1,0,3,2:T(8,128)(2,1)} reshape(bf16[4096,64]{0,1:T(8,128)(2,1)S(1)} %fusion.19) | data formatting | bytes 1048576 | tf_op jit(solution)/shard_map/reshape | solution.py:97
  124.7 13.5 %copy.22 = bf16[32,4,2,1024]{3,2,1,0:T(2,128)(2,1)S(1)} copy(bf16[32,4,2,1024]{1,3,2,0:T(8,128)(2,1)} %bitcast.64) | data formatting | bytes 1048576 | tf_op jit(solution)/shard_map/transpose | solution.py:98
  138.2 0.2 reshape_reshape.3
  138.4 270.9 %while.12 = (s32[]{:T(128)}, f32[8,4,2,512]{3,2,1,0:T(2,128)S(1)}, s32[8,4]{1,0:T(8,128)S(1)}, bf16[8,4,8,1024]{3,2,1,0:T(8,128)(2,1)S(1)}, f32[512]{0:T(512)S(1...) while((s32[]{:T(128)}, f32[8,4,2,512]{3,2,1,0:T(2,128)S(1)}, ...), condition=%wide.region_4.5_spmd.clone.clone, body=%wide.region_1.4_spmd.clone.clone.sunk | while | flops 92858400 | bytes 22143284 | solution.py:122
  138.4 0.4 multiply_add_fusion.2
  138.9 30.2 %fusion.74 = (bf16[4,512,1024]{2,1,0:T(8,128)(2,1)S(1)}, bf16[4,512,1024]{2,1,0:T(8,128)(2,1)S(1)}) fusion(f32[512,1024]{1,0:T(8,128)S(1)} %multiply_add_fusion.2, f32[4]{0:T(128)S(1)} %multiply_bitcast_fusion.4), kind=kLoop, calls=%fused_computation.4.clone.1 | loop fusion | flops 6291456 | bytes 10485776 | tf_op jit(solution)/shard_map/convert
  169.1 2.6 fusion.75
  171.9 0.1 slice_add_fusion.2
  172.2 0.1 reshape_multiply_fusion.3
  172.3 0.4 multiply_add_fusion.2
  172.8 30.2 %fusion.74 = (bf16[4,512,1024]{2,1,0:T(8,128)(2,1)S(1)}, bf16[4,512,1024]{2,1,0:T(8,128)(2,1)S(1)}) fusion(f32[512,1024]{1,0:T(8,128)S(1)} %multiply_add_fusion.2, f32[4]{0:T(128)S(1)} %multiply_bitcast_fusion.4), kind=kLoop, calls=%fused_computation.4.clone.1 | loop fusion | flops 6291456 | bytes 10485776 | tf_op jit(solution)/shard_map/convert
  203.0 2.6 fusion.75
  205.8 0.1 slice_add_fusion.2
  206.0 0.1 reshape_multiply_fusion.3
  206.2 0.4 multiply_add_fusion.2
  206.6 30.2 %fusion.74 = (bf16[4,512,1024]{2,1,0:T(8,128)(2,1)S(1)}, bf16[4,512,1024]{2,1,0:T(8,128)(2,1)S(1)}) fusion(f32[512,1024]{1,0:T(8,128)S(1)} %multiply_add_fusion.2, f32[4]{0:T(128)S(1)} %multiply_bitcast_fusion.4), kind=kLoop, calls=%fused_computation.4.clone.1 | loop fusion | flops 6291456 | bytes 10485776 | tf_op jit(solution)/shard_map/convert
  236.9 2.6 fusion.75
  239.6 0.1 slice_add_fusion.2
  239.9 0.1 reshape_multiply_fusion.3
  240.0 0.4 multiply_add_fusion.2
  240.5 30.2 %fusion.74 = (bf16[4,512,1024]{2,1,0:T(8,128)(2,1)S(1)}, bf16[4,512,1024]{2,1,0:T(8,128)(2,1)S(1)}) fusion(f32[512,1024]{1,0:T(8,128)S(1)} %multiply_add_fusion.2, f32[4]{0:T(128)S(1)} %multiply_bitcast_fusion.4), kind=kLoop, calls=%fused_computation.4.clone.1 | loop fusion | flops 6291456 | bytes 10485776 | tf_op jit(solution)/shard_map/convert
  270.7 2.6 fusion.75
  273.5 0.1 slice_add_fusion.2
  273.7 0.1 reshape_multiply_fusion.3
  273.9 0.4 multiply_add_fusion.2
  274.3 30.2 %fusion.74 = (bf16[4,512,1024]{2,1,0:T(8,128)(2,1)S(1)}, bf16[4,512,1024]{2,1,0:T(8,128)(2,1)S(1)}) fusion(f32[512,1024]{1,0:T(8,128)S(1)} %multiply_add_fusion.2, f32[4]{0:T(128)S(1)} %multiply_bitcast_fusion.4), kind=kLoop, calls=%fused_computation.4.clone.1 | loop fusion | flops 6291456 | bytes 10485776 | tf_op jit(solution)/shard_map/convert
  304.6 2.6 fusion.75
  307.3 0.1 slice_add_fusion.2
  307.7 0.4 multiply_add_fusion.2
  308.2 30.2 %fusion.74 = (bf16[4,512,1024]{2,1,0:T(8,128)(2,1)S(1)}, bf16[4,512,1024]{2,1,0:T(8,128)(2,1)S(1)}) fusion(f32[512,1024]{1,0:T(8,128)S(1)} %multiply_add_fusion.2, f32[4]{0:T(128)S(1)} %multiply_bitcast_fusion.4), kind=kLoop, calls=%fused_computation.4.clone.1 | loop fusion | flops 6291456 | bytes 10485776 | tf_op jit(solution)/shard_map/convert
  338.4 2.6 fusion.75
  341.2 0.1 slice_add_fusion.2
  341.6 0.4 multiply_add_fusion.2
  342.1 30.2 %fusion.74 = (bf16[4,512,1024]{2,1,0:T(8,128)(2,1)S(1)}, bf16[4,512,1024]{2,1,0:T(8,128)(2,1)S(1)}) fusion(f32[512,1024]{1,0:T(8,128)S(1)} %multiply_add_fusion.2, f32[4]{0:T(128)S(1)} %multiply_bitcast_fusion.4), kind=kLoop, calls=%fused_computation.4.clone.1 | loop fusion | flops 6291456 | bytes 10485776 | tf_op jit(solution)/shard_map/convert
  372.3 2.6 fusion.75
  375.1 0.1 slice_add_fusion.2
  375.5 0.4 multiply_add_fusion.2
  375.9 30.2 %fusion.74 = (bf16[4,512,1024]{2,1,0:T(8,128)(2,1)S(1)}, bf16[4,512,1024]{2,1,0:T(8,128)(2,1)S(1)}) fusion(f32[512,1024]{1,0:T(8,128)S(1)} %multiply_add_fusion.2, f32[4]{0:T(128)S(1)} %multiply_bitcast_fusion.4), kind=kLoop, calls=%fused_computation.4.clone.1 | loop fusion | flops 6291456 | bytes 10485776 | tf_op jit(solution)/shard_map/convert
  406.2 2.6 fusion.75
  408.9 0.1 slice_add_fusion.2
  409.3 0.6 copy-done.1
  410.0 1.3 dynamic-slice
  411.3 150.1 %all-reduce.3.cloned.1.call-done = f32[32,2,512]{2,1,0:T(2,128)} async-done(((f32[32,2,512]{2,1,0:T(2,128)}), f32[32,2,512]{2,1,0:T(2,128)}) %all-reduce.3.cloned.1.call-update) | async-done | bytes 131088
  561.4 2.0 dynamic-slice_bitcast_fusion
  (94 shorter events, 3.1 us)
Async XLA Ops:
  6.5 1.6 copy-start
  6.5 28.4 %copy-start.3 = (s32[16]{0:T(128)S(1)}, s32[16]{0:T(128)}, u32[]{:S(2)}) copy-start(s32[16]{0:T(128)} %param.8) | copy-start | bytes 196
  6.5 32.4 %copy-start.2 = (s32[2,512]{1,0:T(2,128)S(1)}, s32[2,512]{1,0:T(2,128)}, u32[]{:S(2)}) copy-start(s32[2,512]{1,0:T(2,128)} %param.9) | copy-start | bytes 12292
  6.5 69.8 %all-gather.2.cloned.1.call-start = ((), (), s32[]{:S(2)}) async-start(), calls=%async_computation.1 | async-start | bytes 4456448 | tf_op jit(solution)/shard_map/all_gather | solution.py:92
  34.9 526.5 %all-reduce.3.cloned.1.call-start = ((), (), s32[]{:S(2)}) async-start(), calls=%async_computation.2 | async-start | bytes 262144
  409.3 0.6 copy-start.1
Sparse Core Ops, SparseCore 0:
  35.0 41.2 all-gather.1
  410.1 151.2 all-reduce.2
where the time goes:
time: 571 us; the launch traced here: 570 us
  other arithmetic  253 us (44%)
  waiting for transfers between devices  187 us (33%)
  local copies, waits for them, and re-layouts  66.6 us (12%)
  matrix products  24.7 us (4%)
  blocking collectives  24.5 us (4%)
  between operations  13.6 us (2%)
    another operation x8, other arithmetic  242 us
    unnamed x3, waiting for transfers between devices  150 us
    all_gather x1, waiting for transfers between devices, per_device(): row_piece = lax.all_gather(arrived, 'nar', axis=0, tiled=True)  37.2 us
    reshape x1, local copies, waits for them, and re-layouts, per_device(): (spectral * dft_scale).astype(jnp.bfloat16)  37.2 us
    all_to_all x1, blocking collectives, per_device(): lax.all_to_all(packed, 'vol', split_axis=0, concat_axis=0, tiled=True)  24.5 us
    dot_general x8, matrix products, apply_green(): jnp.einsum('bxp,bcp->bxc', green_grid, spec_block, preferred_element_type...  21.1 us
    transpose x1, local copies, waits for them, and re-layouts, per_device(): spectra = spectral.transpose(2, 1, 3, 0).reshape(bin_cap, 2 * NQ, rows_here)  13.5 us
  transfers between devices with their start and end apart: 2, of which 2 were waited for; matrix products, arithmetic and copies ran while one was open for 1% of the time, Pallas kernels for 0%

commit v1 on v0

--- a/solution.py
+++ b/solution.py
@@ -89,7 +89,26 @@
     dft_scale = 1.0 / math.sqrt(time_len)
     within = jnp.arange(bin_cap, dtype=jnp.int32)
     own_table = dft_table(own_start + within, within < own_count, time_len)
-    row_piece = lax.all_gather(arrived, "nar", axis=0, tiled=True)
+    devices, position, extent = (lax.axis_size("nar"), lax.axis_index("nar"), arrived.shape[0])
+    right = [(i, (i + 1) % devices) for i in range(devices)]
+    behind = [(i, (i - 1) % devices) for i in range(devices)]
+    whole = jnp.zeros(
+        (*arrived.shape[:0], devices * extent, *arrived.shape[0 + 1 :]), arrived.dtype
+    )
+    whole = lax.dynamic_update_slice_in_dim(whole, arrived, position * extent, axis=0)
+    from_left = from_right = arrived
+    halfway = devices // 2
+    for turn in range(1, halfway + 1):
+        from_left = lax.ppermute(from_left, "nar", right)
+        whole = lax.dynamic_update_slice_in_dim(
+            whole, from_left, (position - turn) % devices * extent, axis=0
+        )
+        if turn < devices - halfway:
+            from_right = lax.ppermute(from_right, "nar", behind)
+            whole = lax.dynamic_update_slice_in_dim(
+                whole, from_right, (position + turn) % devices * extent, axis=0
+            )
+    row_piece = whole
     rows_here = row_piece.shape[0]
     spectral = jnp.dot(
         row_piece.reshape(rows_here * NQ, time_len), own_table, preferred_element_type=jnp.float32

time: 571 us -> 584 us (1.023)
  starting transfers between devices: 0.04 us -> 34.2 us
  blocking collectives: 24.5 us -> 0 us
  local copies, waits for them, and re-layouts: 66.6 us -> 80.6 us
  waiting for transfers between devices: 187 us -> 174 us
    all_gather x1 -> x0, waiting for transfers between devices: 37.2 us -> none  [per_device(): row_piece = lax.all_gather(arrived, 'nar', axis=0, tiled=True)]
    all_to_all x1 -> x0, blocking collectives: 24.5 us -> none  [per_device(): lax.all_to_all(packed, 'vol', split_axis=0, concat_axis=0, tiled=True)]
    ppermute x0 -> x15, waiting for transfers between devices: none -> 21.4 us  [the longest x8 21.4 us: per_device(): from_left = lax.ppermute(from_left, 'nar', right)]
    ppermute x0 -> x15, starting transfers between devices: none -> 20.7 us  [the longest x7 20.7 us: per_device(): from_right = lax.ppermute(from_right, 'nar', behind)]
    all_to_all x0 -> x1, starting transfers between devices: none -> 13.5 us  [per_device(): lax.all_to_all(packed, 'vol', split_axis=0, concat_axis=0, tiled=True)]
    dynamic_update_slice x0 -> x16, local copies, waits for them, and re-layouts: none -> 11.6 us  [the longest x8 5.78 us: per_device(): lax.dynamic_update_slice_in_dim(whole, from_left, (position - turn) % dev...]
    unnamed x3 -> x2, waiting for transfers between devices: 150 us -> 148 us
  transfers between devices with their start and end apart: 2 -> 17, of which waited for: 2 -> 10; matrix products, arithmetic and copies ran while one was open for 1% -> 4% of each run, Pallas kernels for 0% -> 0%
where the time goes in v1:
time: 584 us; the launch traced here: 583 us
  other arithmetic  255 us (44%)
  waiting for transfers between devices  174 us (30%)
  local copies, waits for them, and re-layouts  80.6 us (14%)
  starting transfers between devices  34.2 us (6%)
  matrix products  24.7 us (4%)
  between operations  13.9 us (2%)
    another operation x8, other arithmetic  242 us
    unnamed x2, waiting for transfers between devices  148 us
    reshape x1, local copies, waits for them, and re-layouts, per_device(): (spectral * dft_scale).astype(jnp.bfloat16)  37.2 us
    ppermute x8, waiting for transfers between devices, per_device(): from_left = lax.ppermute(from_left, 'nar', right)  21.4 us
    dot_general x8, matrix products, apply_green(): jnp.einsum('bxp,bcp->bxc', green_grid, spec_block, preferred_element_type...  21.1 us
    ppermute x7, starting transfers between devices, per_device(): from_right = lax.ppermute(from_right, 'nar', behind)  20.7 us
    transpose x1, local copies, waits for them, and re-layouts, per_device(): spectra = spectral.transpose(2, 1, 3, 0).reshape(bin_cap, 2 * NQ, rows_here)  13.5 us
    all_to_all x1, starting transfers between devices, per_device(): lax.all_to_all(packed, 'vol', split_axis=0, concat_axis=0, tiled=True)  13.5 us
  transfers between devices with their start and end apart: 17, of which 10 were waited for; matrix products, arithmetic and copies ran while one was open for 4% of the time, Pallas kernels for 0%

profile of v1, /device:TPU:2, one launch (start us, length us, event | category | flops | bytes accessed | tf_op | source)
XLA Modules:
  0.0 583.3 jit_solution(1949830110664192230)
XLA Ops:
  6.5 0.7 compare_reduce_fusion
  8.2 0.7 gather_fusion
  9.1 1.1 broadcast_select_fusion.1
  10.2 13.5 %all-to-all-start = ((bf16[32,2,2048]{2,1,0:T(2,128)(2,1)}), bf16[32,2,2048]{2,1,0:T(2,128)(2,1)S(1)}, u32[]{:S(2)}, u32[]{:S(2)}) async-start(bf16[32,2,2048]{2,1,0:T(2,128)(2,1)} %broadcast_select_fusion.1), calls=%async_computation | async-start | bytes 524288 | tf_op jit(solution)/shard_map/all_to_all | solution.py:84
  23.7 0.8 select_reduce_fusion
  24.5 1.3 dynamic_slice.15
  27.6 0.9 fusion.58
  28.5 0.7 iota_compare_fusion.1
  29.7 5.3 all-to-all-done
  35.1 2.9 collective-permute-start.1
  38.6 2.5 broadcast_in_dim.78
  41.1 0.7 constant_dynamic-update-slice_fusion.15
  42.1 3.0 collective-permute-start.3
  45.1 0.7 constant_dynamic-update-slice_fusion.14
  45.8 0.7 constant_dynamic-update-slice_fusion.13
  46.5 2.6 collective-permute-done.2
  49.1 3.0 collective-permute-start.5
  52.1 0.7 constant_dynamic-update-slice_fusion.12
  52.8 0.7 constant_dynamic-update-slice_fusion.11
  53.5 2.6 collective-permute-done.4
  56.1 3.0 collective-permute-start.7
  59.1 0.7 constant_dynamic-update-slice_fusion.10
  59.8 0.7 constant_dynamic-update-slice_fusion.9
  60.5 2.6 collective-permute-done.6
  63.1 3.0 collective-permute-start.9
  66.1 0.7 constant_dynamic-update-slice_fusion.8
  66.8 0.7 constant_dynamic-update-slice_fusion.7
  67.5 2.6 collective-permute-done.8
  70.1 3.0 collective-permute-start.11
  73.1 0.7 constant_dynamic-update-slice_fusion.6
  73.8 0.7 constant_dynamic-update-slice_fusion.5
  74.5 2.6 collective-permute-done.10
  77.1 3.0 collective-permute-start.13
  80.1 0.7 constant_dynamic-update-slice_fusion.4
  80.8 0.7 constant_dynamic-update-slice_fusion.3
  81.6 2.6 collective-permute-done.12
  84.2 0.7 constant_dynamic-update-slice_fusion.2
  84.9 0.7 constant_dynamic-update-slice_fusion.1
  85.6 5.5 collective-permute-done.14
  91.2 0.7 constant_dynamic-update-slice_fusion
  91.9 7.6 %reshape.422 = bf16[4096,512]{1,0:T(8,128)(2,1)} reshape(bf16[1024,2048]{1,0:T(8,128)(2,1)} %constant_dynamic-update-slice_fusion) | data formatting | bytes 8388608 | tf_op jit(solution)/shard_map/reshape | solution.py:114
  99.5 3.6 fusion.19
  103.0 37.2 %reshape.423 = bf16[1024,4,32,2]{1,0,3,2:T(8,128)(2,1)} reshape(bf16[4096,64]{0,1:T(8,128)(2,1)S(1)} %fusion.19) | data formatting | bytes 1048576 | tf_op jit(solution)/shard_map/reshape | solution.py:116
  140.2 13.5 %copy.22 = bf16[32,4,2,1024]{3,2,1,0:T(2,128)(2,1)S(1)} copy(bf16[32,4,2,1024]{1,3,2,0:T(8,128)(2,1)} %bitcast.64) | data formatting | bytes 1048576 | tf_op jit(solution)/shard_map/transpose | solution.py:117
  153.9 270.9 %while.12 = (s32[]{:T(128)}, f32[8,4,2,512]{3,2,1,0:T(2,128)S(1)}, s32[8,4]{1,0:T(8,128)S(1)}, bf16[8,4,8,1024]{3,2,1,0:T(8,128)(2,1)S(1)}, f32[512]{0:T(512)S(1...) while((s32[]{:T(128)}, f32[8,4,2,512]{3,2,1,0:T(2,128)S(1)}, ...), condition=%wide.region_4.5_spmd.clone.clone, body=%wide.region_1.4_spmd.clone.clone.sunk | while | flops 92858400 | bytes 22143284 | solution.py:141
  154.4 30.2 %fusion.74 = (bf16[4,512,1024]{2,1,0:T(8,128)(2,1)S(1)}, bf16[4,512,1024]{2,1,0:T(8,128)(2,1)S(1)}) fusion(f32[512,1024]{1,0:T(8,128)S(1)} %multiply_add_fusion.2, f32[4]{0:T(128)S(1)} %multiply_bitcast_fusion.4), kind=kLoop, calls=%fused_computation.4.clone.1 | loop fusion | flops 6291456 | bytes 10485776 | tf_op jit(solution)/shard_map/convert
  184.7 2.6 fusion.75
  188.3 30.2 %fusion.74 = (bf16[4,512,1024]{2,1,0:T(8,128)(2,1)S(1)}, bf16[4,512,1024]{2,1,0:T(8,128)(2,1)S(1)}) fusion(f32[512,1024]{1,0:T(8,128)S(1)} %multiply_add_fusion.2, f32[4]{0:T(128)S(1)} %multiply_bitcast_fusion.4), kind=kLoop, calls=%fused_computation.4.clone.1 | loop fusion | flops 6291456 | bytes 10485776 | tf_op jit(solution)/shard_map/convert
  218.5 2.6 fusion.75
  222.2 30.2 %fusion.74 = (bf16[4,512,1024]{2,1,0:T(8,128)(2,1)S(1)}, bf16[4,512,1024]{2,1,0:T(8,128)(2,1)S(1)}) fusion(f32[512,1024]{1,0:T(8,128)S(1)} %multiply_add_fusion.2, f32[4]{0:T(128)S(1)} %multiply_bitcast_fusion.4), kind=kLoop, calls=%fused_computation.4.clone.1 | loop fusion | flops 6291456 | bytes 10485776 | tf_op jit(solution)/shard_map/convert
  252.4 2.6 fusion.75
  256.0 30.2 %fusion.74 = (bf16[4,512,1024]{2,1,0:T(8,128)(2,1)S(1)}, bf16[4,512,1024]{2,1,0:T(8,128)(2,1)S(1)}) fusion(f32[512,1024]{1,0:T(8,128)S(1)} %multiply_add_fusion.2, f32[4]{0:T(128)S(1)} %multiply_bitcast_fusion.4), kind=kLoop, calls=%fused_computation.4.clone.1 | loop fusion | flops 6291456 | bytes 10485776 | tf_op jit(solution)/shard_map/convert
  286.2 2.6 fusion.75
  289.9 30.2 %fusion.74 = (bf16[4,512,1024]{2,1,0:T(8,128)(2,1)S(1)}, bf16[4,512,1024]{2,1,0:T(8,128)(2,1)S(1)}) fusion(f32[512,1024]{1,0:T(8,128)S(1)} %multiply_add_fusion.2, f32[4]{0:T(128)S(1)} %multiply_bitcast_fusion.4), kind=kLoop, calls=%fused_computation.4.clone.1 | loop fusion | flops 6291456 | bytes 10485776 | tf_op jit(solution)/shard_map/convert
  320.1 2.6 fusion.75
  323.7 30.2 %fusion.74 = (bf16[4,512,1024]{2,1,0:T(8,128)(2,1)S(1)}, bf16[4,512,1024]{2,1,0:T(8,128)(2,1)S(1)}) fusion(f32[512,1024]{1,0:T(8,128)S(1)} %multiply_add_fusion.2, f32[4]{0:T(128)S(1)} %multiply_bitcast_fusion.4), kind=kLoop, calls=%fused_computation.4.clone.1 | loop fusion | flops 6291456 | bytes 10485776 | tf_op jit(solution)/shard_map/convert
  354.0 2.6 fusion.75
  357.6 30.2 %fusion.74 = (bf16[4,512,1024]{2,1,0:T(8,128)(2,1)S(1)}, bf16[4,512,1024]{2,1,0:T(8,128)(2,1)S(1)}) fusion(f32[512,1024]{1,0:T(8,128)S(1)} %multiply_add_fusion.2, f32[4]{0:T(128)S(1)} %multiply_bitcast_fusion.4), kind=kLoop, calls=%fused_computation.4.clone.1 | loop fusion | flops 6291456 | bytes 10485776 | tf_op jit(solution)/shard_map/convert
  387.8 2.6 fusion.75
  391.5 30.2 %fusion.74 = (bf16[4,512,1024]{2,1,0:T(8,128)(2,1)S(1)}, bf16[4,512,1024]{2,1,0:T(8,128)(2,1)S(1)}) fusion(f32[512,1024]{1,0:T(8,128)S(1)} %multiply_add_fusion.2, f32[4]{0:T(128)S(1)} %multiply_bitcast_fusion.4), kind=kLoop, calls=%fused_computation.4.clone.1 | loop fusion | flops 6291456 | bytes 10485776 | tf_op jit(solution)/shard_map/convert
  421.7 2.6 fusion.75
  425.5 1.4 dynamic-slice
  426.9 147.6 %all-reduce.3.cloned.1.call-done = f32[32,2,512]{2,1,0:T(2,128)} async-done(((f32[32,2,512]{2,1,0:T(2,128)}), f32[32,2,512]{2,1,0:T(2,128)}) %all-reduce.3.cloned.1.call-update) | async-done | bytes 131088
  574.5 2.0 dynamic-slice_bitcast_fusion
  (135 shorter events, 12.1 us)
Async XLA Ops:
  6.5 1.6 copy-start
  10.2 24.8 %all-to-all-start = ((bf16[32,2,2048]{2,1,0:T(2,128)(2,1)}), bf16[32,2,2048]{2,1,0:T(2,128)(2,1)S(1)}, u32[]{:S(2)}, u32[]{:S(2)}) async-start(bf16[32,2,2048]{2,1,0:T(2,128)(2,1)} %broadcast_select_fusion.1), calls=%async_computation | async-start | bytes 524288 | tf_op jit(solution)/shard_map/all_to_all | solution.py:84
  23.7 550.8 %all-reduce.3.cloned.1.call-start = ((), (), s32[]{:S(2)}) async-start(), calls=%async_computation.1 | async-start | bytes 262144
  35.1 7.0 %collective-permute-start = (bf16[64,2048]{1,0:T(8,128)(2,1)S(1)}, bf16[64,2048]{1,0:T(8,128)(2,1)S(1)}, u32[]{:S(2)}, u32[]{:S(2)}) collective-permute-start(bf16[64,2048]{1,0:T(8,128)(2,1)S(1)} %all_to_all.7), channel_id=1, source_target_pairs={{0,1},{1,2},{2,3},{3,4},{4,5},{5,6},{6,7},{7,8},{8,9},{9,10},{10,1... | collective-permute-start | bytes 786440 | tf_op jit(solution)/shard_map/ppermute | solution.py:102
  35.1 7.0 %collective-permute-start.1 = (bf16[64,2048]{1,0:T(8,128)(2,1)S(1)}, bf16[64,2048]{1,0:T(8,128)(2,1)S(1)}, u32[]{:S(2)}, u32[]{:S(2)}) collective-permute-start(bf16[64,2048]{1,0:T(8,128)(2,1)S(1)} %all_to_all.7), channel_id=1, source_target_pairs={{0,15},{1,0},{2,1},{3,2},{4,3},{5,4},{6,5},{7,6},{8,7},{9,8},{10,9... | collective-permute-start | bytes 786440 | tf_op jit(solution)/shard_map/ppermute | solution.py:107
  42.1 7.0 %collective-permute-start.2 = (bf16[64,2048]{1,0:T(8,128)(2,1)S(1)}, bf16[64,2048]{1,0:T(8,128)(2,1)S(1)}, u32[]{:S(2)}, u32[]{:S(2)}) collective-permute-start(bf16[64,2048]{1,0:T(8,128)(2,1)S(1)} %collective-permute-done), channel_id=1, source_target_pairs={{0,1},{1,2},{2,3},{3,4},{4,5},{5,6},{6,7},{7,8},{8,9},{9,10},{10,1... | collective-permute-start | bytes 786440 | tf_op jit(solution)/shard_map/ppermute | solution.py:102
  42.1 7.0 %collective-permute-start.3 = (bf16[64,2048]{1,0:T(8,128)(2,1)S(1)}, bf16[64,2048]{1,0:T(8,128)(2,1)S(1)}, u32[]{:S(2)}, u32[]{:S(2)}) collective-permute-start(bf16[64,2048]{1,0:T(8,128)(2,1)S(1)} %collective-permute-done.1), channel_id=1, source_target_pairs={{0,15},{1,0},{2,1},{3,2},{4,3},{5,4},{6,5},{7,6},{8,7},{9,8},{10,9... | collective-permute-start | bytes 786440 | tf_op jit(solution)/shard_map/ppermute | solution.py:107
  49.1 7.0 %collective-permute-start.4 = (bf16[64,2048]{1,0:T(8,128)(2,1)S(1)}, bf16[64,2048]{1,0:T(8,128)(2,1)S(1)}, u32[]{:S(2)}, u32[]{:S(2)}) collective-permute-start(bf16[64,2048]{1,0:T(8,128)(2,1)S(1)} %collective-permute-done.2), channel_id=1, source_target_pairs={{0,1},{1,2},{2,3},{3,4},{4,5},{5,6},{6,7},{7,8},{8,9},{9,10},{10,1... | collective-permute-start | bytes 786440 | tf_op jit(solution)/shard_map/ppermute | solution.py:102
  49.1 7.0 %collective-permute-start.5 = (bf16[64,2048]{1,0:T(8,128)(2,1)S(1)}, bf16[64,2048]{1,0:T(8,128)(2,1)S(1)}, u32[]{:S(2)}, u32[]{:S(2)}) collective-permute-start(bf16[64,2048]{1,0:T(8,128)(2,1)S(1)} %collective-permute-done.3), channel_id=1, source_target_pairs={{0,15},{1,0},{2,1},{3,2},{4,3},{5,4},{6,5},{7,6},{8,7},{9,8},{10,9... | collective-permute-start | bytes 786440 | tf_op jit(solution)/shard_map/ppermute | solution.py:107
  56.1 7.0 %collective-permute-start.6 = (bf16[64,2048]{1,0:T(8,128)(2,1)S(1)}, bf16[64,2048]{1,0:T(8,128)(2,1)S(1)}, u32[]{:S(2)}, u32[]{:S(2)}) collective-permute-start(bf16[64,2048]{1,0:T(8,128)(2,1)S(1)} %collective-permute-done.4), channel_id=1, source_target_pairs={{0,1},{1,2},{2,3},{3,4},{4,5},{5,6},{6,7},{7,8},{8,9},{9,10},{10,1... | collective-permute-start | bytes 786440 | tf_op jit(solution)/shard_map/ppermute | solution.py:102
  56.1 7.0 %collective-permute-start.7 = (bf16[64,2048]{1,0:T(8,128)(2,1)S(1)}, bf16[64,2048]{1,0:T(8,128)(2,1)S(1)}, u32[]{:S(2)}, u32[]{:S(2)}) collective-permute-start(bf16[64,2048]{1,0:T(8,128)(2,1)S(1)} %collective-permute-done.5), channel_id=1, source_target_pairs={{0,15},{1,0},{2,1},{3,2},{4,3},{5,4},{6,5},{7,6},{8,7},{9,8},{10,9... | collective-permute-start | bytes 786440 | tf_op jit(solution)/shard_map/ppermute | solution.py:107
  63.1 7.0 %collective-permute-start.8 = (bf16[64,2048]{1,0:T(8,128)(2,1)S(1)}, bf16[64,2048]{1,0:T(8,128)(2,1)S(1)}, u32[]{:S(2)}, u32[]{:S(2)}) collective-permute-start(bf16[64,2048]{1,0:T(8,128)(2,1)S(1)} %collective-permute-done.6), channel_id=1, source_target_pairs={{0,1},{1,2},{2,3},{3,4},{4,5},{5,6},{6,7},{7,8},{8,9},{9,10},{10,1... | collective-permute-start | bytes 786440 | tf_op jit(solution)/shard_map/ppermute | solution.py:102
  63.1 7.0 %collective-permute-start.9 = (bf16[64,2048]{1,0:T(8,128)(2,1)S(1)}, bf16[64,2048]{1,0:T(8,128)(2,1)S(1)}, u32[]{:S(2)}, u32[]{:S(2)}) collective-permute-start(bf16[64,2048]{1,0:T(8,128)(2,1)S(1)} %collective-permute-done.7), channel_id=1, source_target_pairs={{0,15},{1,0},{2,1},{3,2},{4,3},{5,4},{6,5},{7,6},{8,7},{9,8},{10,9... | collective-permute-start | bytes 786440 | tf_op jit(solution)/shard_map/ppermute | solution.py:107
  70.1 7.0 %collective-permute-start.10 = (bf16[64,2048]{1,0:T(8,128)(2,1)S(1)}, bf16[64,2048]{1,0:T(8,128)(2,1)S(1)}, u32[]{:S(2)}, u32[]{:S(2)}) collective-permute-start(bf16[64,2048]{1,0:T(8,128)(2,1)S(1)} %collective-permute-done.8), channel_id=1, source_target_pairs={{0,1},{1,2},{2,3},{3,4},{4,5},{5,6},{6,7},{7,8},{8,9},{9,10},{10,1... | collective-permute-start | bytes 786440 | tf_op jit(solution)/shard_map/ppermute | solution.py:102
  70.1 7.0 %collective-permute-start.11 = (bf16[64,2048]{1,0:T(8,128)(2,1)S(1)}, bf16[64,2048]{1,0:T(8,128)(2,1)S(1)}, u32[]{:S(2)}, u32[]{:S(2)}) collective-permute-start(bf16[64,2048]{1,0:T(8,128)(2,1)S(1)} %collective-permute-done.9), channel_id=1, source_target_pairs={{0,15},{1,0},{2,1},{3,2},{4,3},{5,4},{6,5},{7,6},{8,7},{9,8},{10,9... | collective-permute-start | bytes 786440 | tf_op jit(solution)/shard_map/ppermute | solution.py:107
  77.1 7.0 %collective-permute-start.12 = (bf16[64,2048]{1,0:T(8,128)(2,1)S(1)}, bf16[64,2048]{1,0:T(8,128)(2,1)S(1)}, u32[]{:S(2)}, u32[]{:S(2)}) collective-permute-start(bf16[64,2048]{1,0:T(8,128)(2,1)S(1)} %collective-permute-done.10), channel_id=1, source_target_pairs={{0,1},{1,2},{2,3},{3,4},{4,5},{5,6},{6,7},{7,8},{8,9},{9,10},{10,1... | collective-permute-start | bytes 786440 | tf_op jit(solution)/shard_map/ppermute | solution.py:102
  77.1 7.7 %collective-permute-start.13 = (bf16[64,2048]{1,0:T(8,128)(2,1)S(1)}, bf16[64,2048]{1,0:T(8,128)(2,1)S(1)}, u32[]{:S(2)}, u32[]{:S(2)}) collective-permute-start(bf16[64,2048]{1,0:T(8,128)(2,1)S(1)} %collective-permute-done.11), channel_id=1, source_target_pairs={{0,15},{1,0},{2,1},{3,2},{4,3},{5,4},{6,5},{7,6},{8,7},{9,8},{10,9... | collective-permute-start | bytes 786440 | tf_op jit(solution)/shard_map/ppermute | solution.py:107
  84.1 7.0 %collective-permute-start.14 = (bf16[64,2048]{1,0:T(8,128)(2,1)S(1)}, bf16[64,2048]{1,0:T(8,128)(2,1)S(1)}, u32[]{:S(2)}, u32[]{:S(2)}) collective-permute-start(bf16[64,2048]{1,0:T(8,128)(2,1)S(1)} %collective-permute-done.12), channel_id=1, source_target_pairs={{0,1},{1,2},{2,3},{3,4},{4,5},{5,6},{6,7},{7,8},{8,9},{9,10},{10,1... | collective-permute-start | bytes 786440 | tf_op jit(solution)/shard_map/ppermute | solution.py:102
  424.8 0.7 copy-start.1
Sparse Core Ops, SparseCore 0:
  425.6 148.7 all-reduce.2
